TPU v7x, 128 devices: a whole 4x4x4 slice. The times are simulated.
128 devices in a mesh: blk: 4 (over x_lo, core), dom: 32 (over z, y, x_hi).
Axes of the slice: x: 4 (x_hi: 2, x_lo: 2; x = x_hi * 2 + x_lo), y: 4, z: 4, core: 2. Of those that a mesh axis runs over, the one named last changes fastest.
Arguments:
- node_feats: bfloat16 [65536, 512], P(('blk', 'dom')), may hold values from -6 to 6
- send_rows: int32 [128, 32, 32], P(('blk', 'dom')), may hold values from 0 to 511
- neighbour_slots: int32 [65536, 8], P(('blk', 'dom')), may hold values from 0 to 1535
- slot_mask: int32 [65536, 8], P(('blk', 'dom')), may hold values 0 or 1
- gate_weight: bfloat16 [512, 512], replicated, may hold values from -0.25 to 0.25
- source_weight: bfloat16 [512, 1024], replicated, may hold values from -0.25 to 0.25
- qkv_weight: bfloat16 [512, 1536], replicated, may hold values from -0.26516504 to 0.26516504
- out_weight: bfloat16 [512, 512], replicated, may hold values from -0.25 to 0.25
- cotangent: bfloat16 [65536, 512], P(('blk', 'dom')), may hold values from -6 to 6
Outputs:
- layer_out: bfloat16 [65536, 512], P(('blk', 'dom'))
- feats_grad: bfloat16 [65536, 512], P(('blk', 'dom'))
- gate_grad: float32 [512, 512], replicated
- source_grad: float32 [512, 1024], replicated
- qkv_grad: float32 [512, 1536], replicated
- out_grad: float32 [512, 512], replicated
Inputs may be any that keep to these rules, and one draw needn't show every extreme that they name: `send_rows`: local node indices of the sending device. `neighbour_slots`: rows below 512 are the device's own nodes, the others received rows.
All inputs are finite; a program needn't handle non-finite values. No bound on the sum of `slot_mask` on one device may be relied on, other than what follows from the above.
Results may differ from a plain program's by a relative error of at most 0.035.
Values may be sent and summed in bfloat16 or wider, within the bound.
No kernel may reach another device: no remote copies, remote signals or barrier semaphores. Data moves between devices by JAX's collectives and lax.ppermute only.
A program may use at most 256 MiB of HBM per device.

v0:
```python
import math
import jax
import jax.numpy as jnp
from jax import lax
from jax.sharding import PartitionSpec as P

HEADS = 8
HDIM = 64


def body(
    node_feats,
    send_rows,
    neighbour_slots,
    slot_mask,
    gate_weight,
    source_weight,
    qkv_weight,
    out_weight,
    cotangent,
):
    node_count, feat_width = node_feats.shape
    head_count = HEADS
    head_width = HDIM
    score_scale = 1.0 / math.sqrt(HDIM)
    peer_count = lax.axis_size("dom")
    outgoing = node_feats[send_rows[0]]
    incoming = lax.all_to_all(outgoing, "dom", split_axis=0, concat_axis=0, tiled=True)
    table = jnp.concatenate([node_feats, incoming.reshape(-1, feat_width)], axis=0)
    table_rows = table.shape[0]
    gate_term = jnp.dot(node_feats, gate_weight, preferred_element_type=jnp.float32)
    source_terms = jnp.dot(table, source_weight, preferred_element_type=jnp.float32)
    edge_source = source_terms[neighbour_slots]
    gate_open = jax.nn.sigmoid(gate_term[:, None, :] + edge_source[:, :, :feat_width])
    edge_value = edge_source[:, :, feat_width:]
    mask_float = slot_mask.astype(jnp.float32)
    slot_weight = mask_float / jnp.maximum(jnp.sum(mask_float, axis=1, keepdims=True), 1.0)
    message = jnp.sum(slot_weight[:, :, None] * gate_open * edge_value, axis=1)
    qkv = jnp.dot(node_feats, qkv_weight, preferred_element_type=jnp.float32).astype(jnp.bfloat16)
    queries = qkv[:, :feat_width].reshape(node_count, head_count, head_width)
    keys_vals = lax.all_gather(qkv[:, feat_width:], "blk", axis=0, tiled=True)
    seq_len = keys_vals.shape[0]
    all_keys = keys_vals[:, :feat_width].reshape(seq_len, head_count, head_width)
    all_values = keys_vals[:, feat_width:].reshape(seq_len, head_count, head_width)
    scores = (
        jnp.einsum("ihe,jhe->hij", queries, all_keys, preferred_element_type=jnp.float32)
        * score_scale
    )
    row_top = jnp.max(scores, axis=2, keepdims=True)
    raw_weights = jnp.exp(scores - row_top)
    row_total = jnp.sum(raw_weights, axis=2, keepdims=True)
    prob_weights = raw_weights / row_total
    prob_half = prob_weights.astype(jnp.bfloat16)
    mixed = (
        jnp.einsum("hij,jhe->ihe", prob_half, all_values, preferred_element_type=jnp.float32)
        .astype(jnp.bfloat16)
        .reshape(node_count, feat_width)
    )
    attended = jnp.dot(mixed, out_weight, preferred_element_type=jnp.float32)
    layer_out = (node_feats.astype(jnp.float32) + message + attended).astype(jnp.bfloat16)
    upstream = cotangent.astype(jnp.float32)
    grad_out_w = jnp.einsum("nd,ne->de", mixed, cotangent, preferred_element_type=jnp.float32)
    d_mixed = jnp.einsum(
        "ne,de->nd", cotangent, out_weight, preferred_element_type=jnp.float32
    ).astype(jnp.bfloat16)
    d_heads = d_mixed.reshape(node_count, head_count, head_width)
    row_delta = jnp.sum(
        d_heads.astype(jnp.float32)
        * mixed.reshape(node_count, head_count, head_width).astype(jnp.float32),
        axis=2,
    )
    d_probs = jnp.einsum("ihe,jhe->hij", d_heads, all_values, preferred_element_type=jnp.float32)
    d_scores = (prob_weights * (d_probs - row_delta.T[:, :, None]) * score_scale).astype(
        jnp.bfloat16
    )
    d_query = jnp.einsum(
        "hij,jhe->ihe", d_scores, all_keys, preferred_element_type=jnp.float32
    ).reshape(node_count, feat_width)
    count = node_count * lax.axis_size("blk")
    d_key = jnp.einsum("hij,ihe->jhe", d_scores, queries, preferred_element_type=jnp.float32)
    d_value = jnp.einsum("hij,ihe->jhe", prob_half, d_heads, preferred_element_type=jnp.float32)
    d_keyval = lax.psum_scatter(
        jnp.concatenate(
            [d_key.reshape(count, feat_width), d_value.reshape(count, feat_width)], axis=1
        ),
        "blk",
        scatter_dimension=0,
        tiled=True,
    )
    d_qkv = jnp.concatenate([d_query, d_keyval], axis=1).astype(jnp.bfloat16)
    grad_qkv_w = jnp.einsum("nd,nf->df", node_feats, d_qkv, preferred_element_type=jnp.float32)
    d_attn_input = jnp.einsum("nf,df->nd", d_qkv, qkv_weight, preferred_element_type=jnp.float32)
    edge_up = slot_weight[:, :, None] * upstream[:, None, :]
    d_edge_value = edge_up * gate_open
    d_edge_logit = edge_up * edge_value * gate_open * (1.0 - gate_open)
    d_gate = jnp.sum(d_edge_logit, axis=1).astype(jnp.bfloat16)
    edge_terms = jnp.concatenate([d_edge_logit, d_edge_value], axis=2).reshape(-1, 2 * feat_width)
    d_source = jax.ops.segment_sum(
        edge_terms, neighbour_slots.reshape(-1), num_segments=table_rows
    ).astype(jnp.bfloat16)
    grad_source_w = jnp.einsum("td,tf->df", table, d_source, preferred_element_type=jnp.float32)
    grad_gate_w = jnp.einsum("nd,nf->df", node_feats, d_gate, preferred_element_type=jnp.float32)
    d_table = jnp.einsum("tf,df->td", d_source, source_weight, preferred_element_type=jnp.float32)
    returned = lax.all_to_all(
        d_table[node_count:].reshape(peer_count, -1, feat_width).astype(jnp.bfloat16),
        "dom",
        split_axis=0,
        concat_axis=0,
        tiled=True,
    ).astype(jnp.float32)
    d_sent = jax.ops.segment_sum(
        returned.reshape(-1, feat_width), send_rows[0].reshape(-1), num_segments=node_count
    )
    d_gate_input = jnp.einsum("nf,df->nd", d_gate, gate_weight, preferred_element_type=jnp.float32)
    feats_grad = (upstream + d_attn_input + d_table[:node_count] + d_gate_input + d_sent).astype(
        jnp.bfloat16
    )
    weight_sums = lax.psum((grad_gate_w, grad_source_w, grad_qkv_w, grad_out_w), ("blk", "dom"))
    return (layer_out, feats_grad, weight_sums[0], weight_sums[1], weight_sums[2], weight_sums[3])


def solution(mesh):
    return jax.shard_map(
        body,
        mesh=mesh,
        in_specs=(
            P(("blk", "dom"), None),
            P(("blk", "dom"), None, None),
            P(("blk", "dom"), None),
            P(("blk", "dom"), None),
            P(),
            P(),
            P(),
            P(),
            P(("blk", "dom"), None),
        ),
        out_specs=(P(("blk", "dom"), None), P(("blk", "dom"), None), P(), P(), P(), P()),
        check_vma=False,
    )
```

profile of v0, /device:TPU:1, one launch (start us, length us, event | category | flops | bytes accessed | tf_op | source)
XLA Modules:
  0.0 508.1 jit_solution(13844792690348114465)
XLA Ops:
  15.5 47.7 %all-gather.2.cloned.1.call-done = bf16[2048,1024]{1,0:T(8,128)(2,1)} async-done(((bf16[512,1024]{1,0:T(8,128)(2,1)}), bf16[2048,1024]{1,0:T(8,128)(2,1)}) %all-gather.2.cloned.1.call-update) | async-done | bytes 4194320 | tf_op jit(solution)/shard_map/all_gather | solution.py:41
  63.2 4.5 fusion.36
  67.7 4.0 copy.28
  71.7 3.9 copy.26
  75.6 16.6 %fusion.37 = (f32[8,512]{1,0:T(8,128)S(1)}, f32[8,512,2048]{2,1,0:T(8,128)}) fusion(bf16[512,8,64]{0,2,1:T(8,128)(2,1)S(1)} %bitcast.82, bf16[2048,8,64]{0,2,1:T(8,128)(2,1)} %bitcast.71), kind=kOutput, calls=%fused_computation.67 | convolution fusion | flops 1098909696 | bytes 36192256 | tf_op jit(solution)/shard_map/sub | solution.py:50
  92.2 19.0 %fusion.8 = bf16[8,512,2048]{2,1,0:T(8,128)(2,1)} fusion(f32[8,512,2048]{2,1,0:T(8,128)} %get-tuple-element.29, f32[8,512]{1,0:T(8,128)S(1)} %get-tuple-element.28), kind=kLoop, calls=%fused_computation.15 | loop fusion | flops 16777216 | bytes 50348032 | tf_op jit(solution)/shard_map/convert_element_type | solution.py:53
  111.3 13.0 %multiply_reduce_fusion.2 = (f32[512,8]{0,1:T(8,128)}, bf16[8,64,512]{2,1,0:T(8,128)(2,1)}) fusion(bf16[512,512]{0,1:T(8,128)(2,1)S(1)} %convolution_convert_fusion.1, bf16[2048,8,64]{0,2,1:T(8,128)(2,1)} %bitcast.73, bf16[8,512,2048]{2,1,0:T(8,128)(2,1)} %fusion.8), kind=kOutput, calls=%fused_computation.49 | convolution fusion | flops 1075048448 | bytes 19939328 | tf_op jit(solution)/shard_map/hij,jhe->ihe/dot_general | solution.py:55
  124.3 10.8 %fusion.40 = f32[8,64,2048]{2,1,0:T(8,128)} fusion(bf16[512,8,64]{0,2,1:T(8,128)(2,1)S(1)} %bitcast.77, bf16[8,512,2048]{2,1,0:T(8,128)(2,1)} %fusion.8), kind=kOutput, calls=%fused_computation.70 | convolution fusion | flops 1073741824 | bytes 21495808 | tf_op jit(solution)/shard_map/hij,ihe->jhe/dot_general | solution.py:81
  135.1 13.4 %multiply_convert_fusion = bf16[8,512,2048]{2,1,0:T(8,128)(2,1)S(1)} fusion(bf16[512,8,64]{0,2,1:T(8,128)(2,1)S(1)} %bitcast.78, bf16[2048,8,64]{0,2,1:T(8,128)(2,1)} %bitcast.74, f32[8,512]{1,0:T(8,128)} %bitcast.85, f32[8,512,2048]{2,1,0:T(8,128)} %get-tuple-element.29, f32[8,512]{1,0:T(8,128)S(1)} %get-tuple-element.28), kind=kOutput, calls=%fused_computation.5 | convolution fusion | flops 1115684864 | bytes 52985856 | tf_op jit(solution)/shard_map/ihe,jhe->hij/dot_general | solution.py:72
  148.5 7.0 %fusion.39 = f32[8,64,2048]{2,1,0:T(8,128)} fusion(bf16[512,8,64]{0,2,1:T(8,128)(2,1)} %bitcast.81, bf16[8,512,2048]{2,1,0:T(8,128)(2,1)S(1)} %multiply_convert_fusion), kind=kOutput, calls=%fused_computation.69 | convolution fusion | flops 1073741824 | bytes 21495808 | tf_op jit(solution)/shard_map/hij,ihe->jhe/dot_general | solution.py:80
  155.5 7.8 %pad_maximum_fusion = f32[2048,1024]{0,1:T(8,128)} fusion(f32[2048,512]{0,1:T(8,128)} %bitcast.69, f32[2048,512]{0,1:T(8,128)} %bitcast.70), kind=kLoop, calls=%fused_computation.25 | loop fusion | flops 2097152 | bytes 16777216 | tf_op jit(solution)/shard_map/concatenate | solution.py:83
  164.3 5.1 gather_fusion
  169.4 9.2 %all-to-all-start = ((bf16[32,32,512]{2,1,0:T(8,128)(2,1)}), bf16[32,32,512]{2,1,0:T(8,128)(2,1)}, u32[]{:S(2)}, u32[]{:S(2)}) async-start(bf16[32,32,512]{2,1,0:T(8,128)(2,1)} %bitcast.79), calls=%async_computation | async-start | bytes 2097152 | tf_op jit(solution)/shard_map/all_to_all | solution.py:28
  183.8 25.8 %all-to-all-done = bf16[32,32,512]{2,1,0:T(8,128)(2,1)} async-done(((bf16[32,32,512]{2,1,0:T(8,128)(2,1)}), bf16[32,32,512]{2,1,0:T(8,128)(2,1)}, u32[]{:S(2)}, u32[]{:S(2)}) %all-to-all-start) | async-done | bytes 1048608 | tf_op jit(solution)/shard_map/all_to_all | solution.py:28
  209.6 6.0 %fusion.26 = f32[1536,1024]{1,0:T(8,128)} fusion(bf16[512,1024]{1,0:T(8,128)(2,1)} %param.14, bf16[1024,512]{1,0:T(8,128)(2,1)} %bitcast.2, bf16[512,512]{1,0:T(8,128)(2,1)S(1)} %copy-done.1), kind=kOutput, calls=%fused_computation.50 | convolution fusion | flops 1613758464 | bytes 8912896 | tf_op jit(solution)/shard_map/dot_general | solution.py:32
  215.6 25.1 %gather_fusion.1 = f32[4096,1024]{1,0:T(8,128)} fusion(f32[1536,1024]{1,0:T(8,128)} %fusion.26, s32[4096]{0:T(1024)S(1)} %broadcast_clamp_fusion), kind=kCustom, calls=%fused_computation.1 | custom fusion | bytes 33570816 | tf_op jit(solution)/shard_map/gather | solution.py:33
  240.7 18.9 %fusion.34 = (bf16[512,512]{1,0:T(8,128)(2,1)S(1)}, f32[512,8,512]{2,1,0:T(8,128)}, f32[512,8,512]{2,1,0:T(8,128)}, f32[512,512]{1,0:T(8,128)}) fusion(f32[512,8,1024]{2,1,0:T(8,128)} %bitcast.68, f32[512,512]{1,0:T(8,128)} %fusion.38, f32[512,512]{1,0:T(8,128)} %convert_element_type.58, f32[512,8]{1,0:T(8,128)S(1)} %copy.24), kind=kLoop, calls=%fused_computation.65 | loop fusion | flops 28835840 | bytes 37240832 | tf_op jit(solution)/shard_map/reduce_sum | solution.py:96
  259.6 38.4 %scatter_custom_fusion = f32[1536,1024]{1,0:T(8,128)} fusion(s32[4096]{0:T(1024)S(1)} %reshape.121, f32[512,8,512]{2,1,0:T(8,128)} %get-tuple-element.24, f32[]{:T(128)} %constant.2.clone.1, f32[512,8,512]{2,1,0:T(8,128)} %get-tuple-element.23, f32[]{:T(128)} %constant.7.clone.1), kind=kCustom, calls=%fused_computation.10 | custom fusion | flops 8388608 | bytes 23068680 | tf_op jit(solution)/shard_map/scatter-add | solution.py:98
  299.5 6.2 %fusion.20 = f32[512,1024]{1,0:T(8,128)} fusion(f32[1536,1024]{1,0:T(8,128)} %scatter_custom_fusion, bf16[1024,512]{1,0:T(8,128)(2,1)} %bitcast.2, bf16[512,512]{1,0:T(8,128)(2,1)S(1)} %copy-done.1), kind=kOutput, calls=%fused_computation.36 | convolution fusion | flops 1615331328 | bytes 9961472 | tf_op jit(solution)/shard_map/td,tf->df/dot_general | solution.py:101
  307.2 12.4 %convolution_convert_fusion.2 = bf16[8,64,512]{2,1,0:T(8,128)(2,1)} fusion(bf16[2048,8,64]{0,2,1:T(8,128)(2,1)} %bitcast.72, bf16[8,512,2048]{2,1,0:T(8,128)(2,1)} %copy-done.2), kind=kOutput, calls=%fused_computation.47 | convolution fusion | flops 1074003968 | bytes 19398656 | tf_op jit(solution)/shard_map/hij,jhe->ihe/dot_general | solution.py:76
  322.3 3.7 convolution_bitcast_fusion
  326.0 4.9 fusion.22
  333.8 4.9 all-to-all-start.1
  338.8 2.9 fusion.25
  341.7 2.8 fusion.24
  346.0 13.1 %all-to-all-done.1 = bf16[32,32,512]{2,1,0:T(8,128)(2,1)} async-done(((bf16[32,32,512]{2,1,0:T(8,128)(2,1)}), bf16[32,32,512]{2,1,0:T(8,128)(2,1)}, u32[]{:S(2)}, u32[]{:S(2)}) %all-to-all-start.1) | async-done | bytes 1048608 | tf_op jit(solution)/shard_map/all_to_all | solution.py:104
  359.0 9.4 %scatter_custom_fusion.1 = f32[512,512]{1,0:T(8,128)} fusion(f32[512,512]{1,0:T(8,128)} %convolution_add_fusion, s32[1024]{0:T(1024)S(1)} %reshape.129, bf16[1024,512]{1,0:T(8,128)(2,1)} %bitcast.26), kind=kCustom, calls=%fused_computation.32 | custom fusion | flops 1048576 | bytes 2097152 | tf_op jit(solution)/shard_map/scatter-add | solution.py:111
  368.4 2.1 convert_element_type.66
  370.6 120.5 %all-reduce.3.cloned.1.call-done = (f32[512,512]{0,1:T(8,128)}, f32[512,1024]{1,0:T(8,128)}, f32[512,1536]{0,1:T(8,128)}, f32[512,512]{1,0:T(8,128)}) async-done(((f32[512,512]{0,1:T(8,128)}, f32[512,1024]{1,0:T(8,128)}, f32[512,1536]{0,1:T(8,128)}, f32[512,512]{1,0:T(8,128)}), (f32[512,512]{0,1:T(8,128)}, f32[512,1024]{1,0:T(8,128)}, f32[512,1536]{0,1:T(8,128)}, ...) | async-done | bytes 7340048 | tf_op jit(solution)/shard_map/psum | solution.py:118
  491.0 2.6 copy.30
  493.6 3.5 copy.31
  497.2 3.2 copy.37
  (66 shorter events, 25.3 us)
Async XLA Ops:
  7.2 1.4 copy-start
  7.2 7.8 %copy-start.3 = (bf16[512,512]{1,0:T(8,128)(2,1)S(1)}, bf16[512,512]{1,0:T(8,128)(2,1)}, u32[]{:S(2)}) copy-start(bf16[512,512]{1,0:T(8,128)(2,1)} %param.17) | copy-start | bytes 1572868
  7.2 7.8 %copy-start.5 = (bf16[512,512]{1,0:T(8,128)(2,1)S(1)}, bf16[512,512]{1,0:T(8,128)(2,1)}, u32[]{:S(2)}) copy-start(bf16[512,512]{1,0:T(8,128)(2,1)} %param.16) | copy-start | bytes 1572868
  7.2 56.0 %all-gather.2.cloned.1.call-start = ((), (), s32[]{:S(2)}) async-start(), calls=%async_computation.3 | async-start | bytes 5242880 | tf_op jit(solution)/shard_map/all_gather | solution.py:41
  10.6 1.1 copy-start.9
  12.9 306.7 %reduce-scatter.2.cloned.1.call-start = ((), (), s32[]{:S(2)}) async-start(), calls=%async_computation.4 | async-start | bytes 10485760 | tf_op jit(solution)/shard_map/reduce_scatter | solution.py:82
  67.7 7.9 %copy-start.8 = (bf16[512,512]{0,1:T(8,128)(2,1)S(1)}, bf16[512,512]{0,1:T(8,128)(2,1)}, u32[]{:S(2)}) copy-start(bf16[512,512]{0,1:T(8,128)(2,1)} %copy.27) | copy-start | bytes 1572868
  148.5 7.0 %copy-start.2 = (bf16[8,512,2048]{2,1,0:T(8,128)(2,1)}, bf16[8,512,2048]{2,1,0:T(8,128)(2,1)S(1)}, u32[]{:S(2)}) copy-start(bf16[8,512,2048]{2,1,0:T(8,128)(2,1)S(1)} %multiply_convert_fusion) | copy-start | bytes 50331652
  163.3 0.7 copy-start.14
  163.3 1.1 copy-start.1
  164.3 15.7 %copy-start.13 = (s32[512,8]{0,1:T(8,128)S(1)}, s32[512,8]{0,1:T(8,128)}, u32[]{:S(2)}) copy-start(s32[512,8]{0,1:T(8,128)} %param.11) | copy-start | bytes 49156
  164.3 16.8 %copy-start.15 = (s32[512,8]{0,1:T(8,128)S(1)}, s32[512,8]{0,1:T(8,128)}, u32[]{:S(2)}) copy-start(s32[512,8]{0,1:T(8,128)} %param.12) | copy-start | bytes 49156
  164.3 18.1 %copy-start.6 = (bf16[512,512]{1,0:T(8,128)(2,1)S(1)}, bf16[512,512]{1,0:T(8,128)(2,1)}, u32[]{:S(2)}) copy-start(bf16[512,512]{1,0:T(8,128)(2,1)} %param.13) | copy-start | bytes 1572868
  169.4 40.2 %all-to-all-start = ((bf16[32,32,512]{2,1,0:T(8,128)(2,1)}), bf16[32,32,512]{2,1,0:T(8,128)(2,1)}, u32[]{:S(2)}, u32[]{:S(2)}) async-start(bf16[32,32,512]{2,1,0:T(8,128)(2,1)} %bitcast.79), calls=%async_computation | async-start | bytes 2097152 | tf_op jit(solution)/shard_map/all_to_all | solution.py:28
  178.7 312.4 %all-reduce.3.cloned.1.call-start = ((), (), s32[]{:S(2)}) async-start(), calls=%async_computation.5 | async-start | bytes 14680064 | tf_op jit(solution)/shard_map/psum | solution.py:118
  298.1 7.7 %copy-start.4 = (bf16[8,64,512]{2,1,0:T(8,128)(2,1)S(1)}, bf16[8,64,512]{2,1,0:T(8,128)(2,1)}, u32[]{:S(2)}) copy-start(bf16[8,64,512]{2,1,0:T(8,128)(2,1)} %get-tuple-element.31) | copy-start | bytes 1572868
  321.3 1.0 copy-start.10
  331.0 1.7 copy-start.12
  333.8 25.3 %all-to-all-start.1 = ((bf16[32,32,512]{2,1,0:T(8,128)(2,1)}), bf16[32,32,512]{2,1,0:T(8,128)(2,1)}, u32[]{:S(2)}, u32[]{:S(2)}) async-start(bf16[32,32,512]{2,1,0:T(8,128)(2,1)} %bitcast.80), calls=%async_computation.2 | async-start | bytes 2097152 | tf_op jit(solution)/shard_map/all_to_all | solution.py:104
  338.8 5.7 %copy-start.7 = (bf16[512,512]{1,0:T(8,128)(2,1)S(1)}, bf16[512,512]{1,0:T(8,128)(2,1)}, u32[]{:S(2)}) copy-start(bf16[512,512]{1,0:T(8,128)(2,1)} %param.13) | copy-start | bytes 1572868
  491.0 9.3 %copy-start.11 = (f32[512,512]{1,0:T(8,128)S(1)}, f32[512,512]{1,0:T(8,128)}, u32[]{:S(2)}) copy-start(f32[512,512]{1,0:T(8,128)} %get-tuple-element.37) | copy-start | bytes 3145732
Sparse Core Ops, SparseCore 0:
  13.0 50.1 all-gather.1
  163.4 90.9 reduce-scatter.1
  326.2 164.8 all-reduce.2
where the time goes:
time: 515 us; the launch traced here: 508 us
  waiting for transfers between devices  207 us (40%)
  matrix products  108 us (21%)
  other arithmetic  98.5 us (19%)
  local copies, waits for them, and re-layouts  65.8 us (13%)
  starting transfers between devices  14.4 us (3%)
  between operations  14.2 us (3%)
    psum x1, waiting for transfers between devices, body(): lax.psum((grad_gate_w, grad_source_w, grad_qkv_w, grad_out_w), ('blk', 'd...  120 us
    all_gather x1, waiting for transfers between devices, body(): keys_vals = lax.all_gather(qkv[:, feat_width:], 'blk', axis=0, tiled=True)  47.7 us
    scatter-add x1, other arithmetic, body(): jax.ops.segment_sum(edge_terms, neighbour_slots.reshape(-1), num_segments...  38.4 us
    all_to_all x1, waiting for transfers between devices, body(): lax.all_to_all(outgoing, 'dom', split_axis=0, concat_axis=0, tiled=True)  25.8 us
    gather x1, local copies, waits for them, and re-layouts, body(): edge_source = source_terms[neighbour_slots]  25.1 us
    convert_element_type x1, other arithmetic, body(): prob_half = prob_weights.astype(jnp.bfloat16)  19 us
    reduce_sum x1, other arithmetic, body(): d_gate = jnp.sum(d_edge_logit, axis=1).astype(jnp.bfloat16)  18.9 us
    unnamed x37, local copies, waits for them, and re-layouts  17.2 us
  transfers between devices with their start and end apart: 5, of which 4 were waited for; matrix products, arithmetic and copies ran while one was open for 29% of the time, Pallas kernels for 0%

commit v1 on v0

--- a/solution.py
+++ b/solution.py
@@ -38,7 +38,9 @@
     message = jnp.sum(slot_weight[:, :, None] * gate_open * edge_value, axis=1)
     qkv = jnp.dot(node_feats, qkv_weight, preferred_element_type=jnp.float32).astype(jnp.bfloat16)
     queries = qkv[:, :feat_width].reshape(node_count, head_count, head_width)
-    keys_vals = lax.all_gather(qkv[:, feat_width:], "blk", axis=0, tiled=True)
+    keys_vals = jnp.concatenate(
+        lax.all_to_all(jnp.stack([qkv[:, feat_width:]] * lax.axis_size("blk")), "blk", 0, 0), axis=0
+    )
     seq_len = keys_vals.shape[0]
     all_keys = keys_vals[:, :feat_width].reshape(seq_len, head_count, head_width)
     all_values = keys_vals[:, feat_width:].reshape(seq_len, head_count, head_width)

time: 515 us -> 532 us (1.033)
  local copies, waits for them, and re-layouts: 65.8 us -> 75.2 us
  starting transfers between devices: 14.4 us -> 22.2 us
    all_gather x1 -> x0, waiting for transfers between devices: 47.7 us -> none  [body(): keys_vals = lax.all_gather(qkv[:, feat_width:], 'blk', axis=0, tiled=True)]
    all_to_all x0 -> x1, waiting for transfers between devices: none -> 45.9 us  [body(): lax.all_to_all(jnp.stack([qkv[:, feat_width:]] * lax.axis_size('blk')), '...]
    all_to_all x0 -> x1, starting transfers between devices: none -> 6.35 us  [body(): lax.all_to_all(jnp.stack([qkv[:, feat_width:]] * lax.axis_size('blk')), '...]
    all_to_all x0 -> x1, local copies, waits for them, and re-layouts: none -> 6.3 us  [body(): lax.all_to_all(jnp.stack([qkv[:, feat_width:]] * lax.axis_size('blk')), '...]
  transfers between devices with their start and end apart: 5 -> 5, of which waited for: 4 -> 4; matrix products, arithmetic and copies ran while one was open for 29% -> 28% of each run, Pallas kernels for 0% -> 0%
where the time goes in v1:
time: 532 us; the launch traced here: 525 us
  waiting for transfers between devices  206 us (39%)
  matrix products  108 us (20%)
  other arithmetic  98.6 us (19%)
  local copies, waits for them, and re-layouts  75.2 us (14%)
  starting transfers between devices  22.2 us (4%)
  between operations  14.5 us (3%)
    psum x1, waiting for transfers between devices, body(): lax.psum((grad_gate_w, grad_source_w, grad_qkv_w, grad_out_w), ('blk', 'd...  122 us
    all_to_all x1, waiting for transfers between devices, body(): lax.all_to_all(jnp.stack([qkv[:, feat_width:]] * lax.axis_size('blk')), '...  45.9 us
    scatter-add x1, other arithmetic, body(): jax.ops.segment_sum(edge_terms, neighbour_slots.reshape(-1), num_segments...  38.4 us
    gather x1, local copies, waits for them, and re-layouts, body(): edge_source = source_terms[neighbour_slots]  25.4 us
    all_to_all x1, waiting for transfers between devices, body(): lax.all_to_all(outgoing, 'dom', split_axis=0, concat_axis=0, tiled=True)  25.1 us
    convert_element_type x1, other arithmetic, body(): prob_half = prob_weights.astype(jnp.bfloat16)  19 us
    reduce_sum x1, other arithmetic, body(): d_gate = jnp.sum(d_edge_logit, axis=1).astype(jnp.bfloat16)  19 us
    unnamed x37, local copies, waits for them, and re-layouts  17.3 us
  transfers between devices with their start and end apart: 5, of which 4 were waited for; matrix products, arithmetic and copies ran while one was open for 28% of the time, Pallas kernels for 0%

profile of v1, /device:TPU:1, one launch (start us, length us, event | category | flops | bytes accessed | tf_op | source)
XLA Modules:
  0.0 524.7 jit_solution(7222098018229012060)
XLA Ops:
  16.7 6.3 %all-to-all-start.1 = ((bf16[4,512,1024]{1,2,0:T(8,128)(2,1)}), bf16[4,512,1024]{1,2,0:T(8,128)(2,1)}, u32[]{:S(2)}, u32[]{:S(2)}) async-start(bf16[4,512,1024]{1,2,0:T(8,128)(2,1)} %stack.2), calls=%async_computation.1 | async-start | bytes 8388608 | tf_op jit(solution)/shard_map/all_to_all | solution.py:42
  24.5 45.9 %all-to-all-done.1 = bf16[4,512,1024]{1,2,0:T(8,128)(2,1)} async-done(((bf16[4,512,1024]{1,2,0:T(8,128)(2,1)}), bf16[4,512,1024]{1,2,0:T(8,128)(2,1)}, u32[]{:S(2)}, u32[]{:S(2)}) %all-to-all-start.1) | async-done | bytes 4194336 | tf_op jit(solution)/shard_map/all_to_all | solution.py:42
  70.4 6.3 %copy.38 = bf16[4,512,1024]{2,1,0:T(8,128)(2,1)} copy(bf16[4,512,1024]{1,2,0:T(8,128)(2,1)} %all-to-all-done.1) | data formatting | bytes 8388608 | tf_op jit(solution)/shard_map/all_to_all | solution.py:42
  76.7 4.5 fusion.36
  81.2 4.0 copy.41
  85.3 3.9 copy.39
  89.2 16.6 %fusion.37 = (f32[8,512]{1,0:T(8,128)S(1)}, f32[8,512,2048]{2,1,0:T(8,128)}) fusion(bf16[512,8,64]{0,2,1:T(8,128)(2,1)S(1)} %bitcast.84, bf16[2048,8,64]{0,2,1:T(8,128)(2,1)} %bitcast.73), kind=kOutput, calls=%fused_computation.67 | convolution fusion | flops 1098909696 | bytes 36192256 | tf_op jit(solution)/shard_map/sub | solution.py:52
  105.8 19.0 %fusion.8 = bf16[8,512,2048]{2,1,0:T(8,128)(2,1)} fusion(f32[8,512,2048]{2,1,0:T(8,128)} %get-tuple-element.41, f32[8,512]{1,0:T(8,128)S(1)} %get-tuple-element.40), kind=kLoop, calls=%fused_computation.15 | loop fusion | flops 16777216 | bytes 50348032 | tf_op jit(solution)/shard_map/convert_element_type | solution.py:55
  124.9 13.0 %multiply_reduce_fusion.2 = (f32[512,8]{0,1:T(8,128)}, bf16[8,64,512]{2,1,0:T(8,128)(2,1)}) fusion(bf16[512,512]{0,1:T(8,128)(2,1)S(1)} %convolution_convert_fusion.1, bf16[2048,8,64]{0,2,1:T(8,128)(2,1)} %bitcast.75, bf16[8,512,2048]{2,1,0:T(8,128)(2,1)} %fusion.8), kind=kOutput, calls=%fused_computation.49 | convolution fusion | flops 1075048448 | bytes 19939328 | tf_op jit(solution)/shard_map/hij,jhe->ihe/dot_general | solution.py:57
  137.9 10.8 %fusion.40 = f32[8,64,2048]{2,1,0:T(8,128)} fusion(bf16[512,8,64]{0,2,1:T(8,128)(2,1)S(1)} %bitcast.79, bf16[8,512,2048]{2,1,0:T(8,128)(2,1)} %fusion.8), kind=kOutput, calls=%fused_computation.70 | convolution fusion | flops 1073741824 | bytes 21495808 | tf_op jit(solution)/shard_map/hij,ihe->jhe/dot_general | solution.py:83
  148.7 13.4 %multiply_convert_fusion = bf16[8,512,2048]{2,1,0:T(8,128)(2,1)S(1)} fusion(bf16[512,8,64]{0,2,1:T(8,128)(2,1)S(1)} %bitcast.80, bf16[2048,8,64]{0,2,1:T(8,128)(2,1)} %bitcast.76, f32[8,512]{1,0:T(8,128)} %bitcast.87, f32[8,512,2048]{2,1,0:T(8,128)} %get-tuple-element.41, f32[8,512]{1,0:T(8,128)S(1)} %get-tuple-element.40), kind=kOutput, calls=%fused_computation.5 | convolution fusion | flops 1115684864 | bytes 52985856 | tf_op jit(solution)/shard_map/ihe,jhe->hij/dot_general | solution.py:74
  162.1 7.0 %fusion.39 = f32[8,64,2048]{2,1,0:T(8,128)} fusion(bf16[512,8,64]{0,2,1:T(8,128)(2,1)} %bitcast.83, bf16[8,512,2048]{2,1,0:T(8,128)(2,1)S(1)} %multiply_convert_fusion), kind=kOutput, calls=%fused_computation.69 | convolution fusion | flops 1073741824 | bytes 21495808 | tf_op jit(solution)/shard_map/hij,ihe->jhe/dot_general | solution.py:82
  169.1 7.8 %pad_maximum_fusion = f32[2048,1024]{0,1:T(8,128)} fusion(f32[2048,512]{0,1:T(8,128)} %bitcast.71, f32[2048,512]{0,1:T(8,128)} %bitcast.72), kind=kLoop, calls=%fused_computation.25 | loop fusion | flops 2097152 | bytes 16777216 | tf_op jit(solution)/shard_map/concatenate | solution.py:85
  177.9 5.1 gather_fusion
  183.0 10.7 %all-to-all-start = ((bf16[32,32,512]{2,1,0:T(8,128)(2,1)}), bf16[32,32,512]{2,1,0:T(8,128)(2,1)}, u32[]{:S(2)}, u32[]{:S(2)}) async-start(bf16[32,32,512]{2,1,0:T(8,128)(2,1)} %bitcast.81), calls=%async_computation | async-start | bytes 2097152 | tf_op jit(solution)/shard_map/all_to_all | solution.py:28
  198.9 25.1 %all-to-all-done = bf16[32,32,512]{2,1,0:T(8,128)(2,1)} async-done(((bf16[32,32,512]{2,1,0:T(8,128)(2,1)}), bf16[32,32,512]{2,1,0:T(8,128)(2,1)}, u32[]{:S(2)}, u32[]{:S(2)}) %all-to-all-start) | async-done | bytes 1048608 | tf_op jit(solution)/shard_map/all_to_all | solution.py:28
  224.0 6.0 %fusion.26 = f32[1536,1024]{1,0:T(8,128)} fusion(bf16[512,1024]{1,0:T(8,128)(2,1)} %param.14, bf16[1024,512]{1,0:T(8,128)(2,1)} %bitcast.2, bf16[512,512]{1,0:T(8,128)(2,1)S(1)} %copy-done.1), kind=kOutput, calls=%fused_computation.50 | convolution fusion | flops 1613758464 | bytes 8912896 | tf_op jit(solution)/shard_map/dot_general | solution.py:32
  230.0 25.4 %gather_fusion.1 = f32[4096,1024]{1,0:T(8,128)} fusion(f32[1536,1024]{1,0:T(8,128)} %fusion.26, s32[4096]{0:T(1024)S(1)} %broadcast_clamp_fusion), kind=kCustom, calls=%fused_computation.1 | custom fusion | bytes 33570816 | tf_op jit(solution)/shard_map/gather | solution.py:33
  255.4 19.0 %fusion.34 = (bf16[512,512]{1,0:T(8,128)(2,1)S(1)}, f32[512,8,512]{2,1,0:T(8,128)}, f32[512,8,512]{2,1,0:T(8,128)}, f32[512,512]{1,0:T(8,128)}) fusion(f32[512,8,1024]{2,1,0:T(8,128)} %bitcast.69, f32[512,512]{1,0:T(8,128)} %fusion.38, f32[512,512]{1,0:T(8,128)} %convert_element_type.58, f32[512,8]{1,0:T(8,128)S(1)} %copy.35), kind=kLoop, calls=%fused_computation.65 | loop fusion | flops 28835840 | bytes 37240832 | tf_op jit(solution)/shard_map/reduce_sum | solution.py:98
  274.4 38.4 %scatter_custom_fusion = f32[1536,1024]{1,0:T(8,128)} fusion(s32[4096]{0:T(1024)S(1)} %reshape.127, f32[512,8,512]{2,1,0:T(8,128)} %get-tuple-element.36, f32[]{:T(128)} %constant.2.clone.1, f32[512,8,512]{2,1,0:T(8,128)} %get-tuple-element.35, f32[]{:T(128)} %constant.7.clone.1), kind=kCustom, calls=%fused_computation.10 | custom fusion | flops 8388608 | bytes 23068680 | tf_op jit(solution)/shard_map/scatter-add | solution.py:100
  314.3 6.2 %fusion.20 = f32[512,1024]{1,0:T(8,128)} fusion(f32[1536,1024]{1,0:T(8,128)} %scatter_custom_fusion, bf16[1024,512]{1,0:T(8,128)(2,1)} %bitcast.2, bf16[512,512]{1,0:T(8,128)(2,1)S(1)} %copy-done.1), kind=kOutput, calls=%fused_computation.36 | convolution fusion | flops 1615331328 | bytes 9961472 | tf_op jit(solution)/shard_map/td,tf->df/dot_general | solution.py:103
  322.0 12.4 %convolution_convert_fusion.2 = bf16[8,64,512]{2,1,0:T(8,128)(2,1)} fusion(bf16[2048,8,64]{0,2,1:T(8,128)(2,1)} %bitcast.74, bf16[8,512,2048]{2,1,0:T(8,128)(2,1)} %copy-done.2), kind=kOutput, calls=%fused_computation.47 | convolution fusion | flops 1074003968 | bytes 19398656 | tf_op jit(solution)/shard_map/hij,jhe->ihe/dot_general | solution.py:78
  337.1 3.7 convolution_bitcast_fusion
  340.8 4.9 fusion.22
  348.6 4.9 all-to-all-start.2
  353.6 2.9 fusion.25
  356.5 2.8 fusion.24
  360.7 12.7 %all-to-all-done.2 = bf16[32,32,512]{2,1,0:T(8,128)(2,1)} async-done(((bf16[32,32,512]{2,1,0:T(8,128)(2,1)}), bf16[32,32,512]{2,1,0:T(8,128)(2,1)}, u32[]{:S(2)}, u32[]{:S(2)}) %all-to-all-start.2) | async-done | bytes 1048608 | tf_op jit(solution)/shard_map/all_to_all | solution.py:106
  373.4 9.4 %scatter_custom_fusion.1 = f32[512,512]{1,0:T(8,128)} fusion(f32[512,512]{1,0:T(8,128)} %convolution_add_fusion, s32[1024]{0:T(1024)S(1)} %reshape.135, bf16[1024,512]{1,0:T(8,128)(2,1)} %bitcast.27), kind=kCustom, calls=%fused_computation.32 | custom fusion | flops 1048576 | bytes 2097152 | tf_op jit(solution)/shard_map/scatter-add | solution.py:113
  384.9 122.4 %all-reduce.3.cloned.1.call-done = (f32[512,512]{0,1:T(8,128)}, f32[512,1024]{1,0:T(8,128)}, f32[512,1536]{0,1:T(8,128)}, f32[512,512]{1,0:T(8,128)}) async-done(((f32[512,512]{0,1:T(8,128)}, f32[512,1024]{1,0:T(8,128)}, f32[512,1536]{0,1:T(8,128)}, f32[512,512]{1,0:T(8,128)}), (f32[512,512]{0,1:T(8,128)}, f32[512,1024]{1,0:T(8,128)}, f32[512,1536]{0,1:T(8,128)}, ...) | async-done | bytes 7340048 | tf_op jit(solution)/shard_map/psum | solution.py:120
  509.9 3.5 copy.44
  513.4 3.2 copy.50
  (69 shorter events, 32.7 us)
Async XLA Ops:
  7.2 1.4 copy-start
  10.6 1.1 copy-start.6
  14.3 8.7 %slice-start = ((bf16[512,1536]{1,0:T(8,128)(2,1)}), bf16[512,512]{1,0:T(8,128)(2,1)S(1)}, s32[]{:S(2)}) async-start(bf16[512,1536]{1,0:T(8,128)(2,1)} %copy-done.6), calls=%async_computation.6 | async-start | bytes 1048576 | tf_op jit(solution)/shard_map/slice | solution.py:40
  16.7 7.4 %copy-start.3 = (bf16[512,512]{1,0:T(8,128)(2,1)S(1)}, bf16[512,512]{1,0:T(8,128)(2,1)}, u32[]{:S(2)}) copy-start(bf16[512,512]{1,0:T(8,128)(2,1)} %param.17) | copy-start | bytes 1572868
  16.7 7.4 %copy-start.5 = (bf16[512,512]{1,0:T(8,128)(2,1)S(1)}, bf16[512,512]{1,0:T(8,128)(2,1)}, u32[]{:S(2)}) copy-start(bf16[512,512]{1,0:T(8,128)(2,1)} %param.16) | copy-start | bytes 1572868
  16.7 53.8 %all-to-all-start.1 = ((bf16[4,512,1024]{1,2,0:T(8,128)(2,1)}), bf16[4,512,1024]{1,2,0:T(8,128)(2,1)}, u32[]{:S(2)}, u32[]{:S(2)}) async-start(bf16[4,512,1024]{1,2,0:T(8,128)(2,1)} %stack.2), calls=%async_computation.1 | async-start | bytes 8388608 | tf_op jit(solution)/shard_map/all_to_all | solution.py:42
  23.0 311.4 %reduce-scatter.2.cloned.1.call-start = ((), (), s32[]{:S(2)}) async-start(), calls=%async_computation.4 | async-start | bytes 10485760 | tf_op jit(solution)/shard_map/reduce_scatter | solution.py:84
  81.2 7.9 %copy-start.9 = (bf16[512,512]{0,1:T(8,128)(2,1)S(1)}, bf16[512,512]{0,1:T(8,128)(2,1)}, u32[]{:S(2)}) copy-start(bf16[512,512]{0,1:T(8,128)(2,1)} %copy.40) | copy-start | bytes 1572868
  162.1 7.0 %copy-start.2 = (bf16[8,512,2048]{2,1,0:T(8,128)(2,1)}, bf16[8,512,2048]{2,1,0:T(8,128)(2,1)S(1)}, u32[]{:S(2)}) copy-start(bf16[8,512,2048]{2,1,0:T(8,128)(2,1)S(1)} %multiply_convert_fusion) | copy-start | bytes 50331652
  176.9 0.7 copy-start.14
  176.9 1.1 copy-start.1
  177.9 17.1 %copy-start.13 = (s32[512,8]{0,1:T(8,128)S(1)}, s32[512,8]{0,1:T(8,128)}, u32[]{:S(2)}) copy-start(s32[512,8]{0,1:T(8,128)} %param.11) | copy-start | bytes 49156
  177.9 18.3 %copy-start.15 = (s32[512,8]{0,1:T(8,128)S(1)}, s32[512,8]{0,1:T(8,128)}, u32[]{:S(2)}) copy-start(s32[512,8]{0,1:T(8,128)} %param.12) | copy-start | bytes 49156
  177.9 19.6 %copy-start.7 = (bf16[512,512]{1,0:T(8,128)(2,1)S(1)}, bf16[512,512]{1,0:T(8,128)(2,1)}, u32[]{:S(2)}) copy-start(bf16[512,512]{1,0:T(8,128)(2,1)} %param.13) | copy-start | bytes 1572868
  183.0 41.0 %all-to-all-start = ((bf16[32,32,512]{2,1,0:T(8,128)(2,1)}), bf16[32,32,512]{2,1,0:T(8,128)(2,1)}, u32[]{:S(2)}, u32[]{:S(2)}) async-start(bf16[32,32,512]{2,1,0:T(8,128)(2,1)} %bitcast.81), calls=%async_computation | async-start | bytes 2097152 | tf_op jit(solution)/shard_map/all_to_all | solution.py:28
  193.7 313.5 %all-reduce.3.cloned.1.call-start = ((), (), s32[]{:S(2)}) async-start(), calls=%async_computation.5 | async-start | bytes 14680064 | tf_op jit(solution)/shard_map/psum | solution.py:120
  312.8 7.7 %copy-start.4 = (bf16[8,64,512]{2,1,0:T(8,128)(2,1)S(1)}, bf16[8,64,512]{2,1,0:T(8,128)(2,1)}, u32[]{:S(2)}) copy-start(bf16[8,64,512]{2,1,0:T(8,128)(2,1)} %get-tuple-element.43) | copy-start | bytes 1572868
  336.1 1.0 copy-start.10
  345.8 1.7 copy-start.12
  348.6 24.9 %all-to-all-start.2 = ((bf16[32,32,512]{2,1,0:T(8,128)(2,1)}), bf16[32,32,512]{2,1,0:T(8,128)(2,1)}, u32[]{:S(2)}, u32[]{:S(2)}) async-start(bf16[32,32,512]{2,1,0:T(8,128)(2,1)} %bitcast.82), calls=%async_computation.3 | async-start | bytes 2097152 | tf_op jit(solution)/shard_map/all_to_all | solution.py:106
  353.6 5.7 %copy-start.8 = (bf16[512,512]{1,0:T(8,128)(2,1)S(1)}, bf16[512,512]{1,0:T(8,128)(2,1)}, u32[]{:S(2)}) copy-start(bf16[512,512]{1,0:T(8,128)(2,1)} %param.13) | copy-start | bytes 1572868
  507.3 9.3 %copy-start.11 = (f32[512,512]{1,0:T(8,128)S(1)}, f32[512,512]{1,0:T(8,128)}, u32[]{:S(2)}) copy-start(f32[512,512]{1,0:T(8,128)} %get-tuple-element.49) | copy-start | bytes 3145732
Sparse Core Ops, SparseCore 0:
  177.0 93.1 reduce-scatter.1
  341.0 166.2 all-reduce.2
